TPU v7x, 256 devices: a whole 4x4x8 slice. The times are simulated.
256 devices in a mesh: vocab: 64 (over z, y, core), rows: 4 (over x).
Axes of the slice: x: 4, y: 4, z: 8, core: 2. Of those that a mesh axis runs over, the one named last changes fastest.
Arguments:
- hidden: bfloat16 [2048, 2880], P('rows'), may hold values from -60 to 60, as said below
- head_weight: bfloat16 [2880, 106496], P(None, ('vocab', 'rows')), may hold values from -0.1118034 to 0.1118034, as said below
- eta_level: float32 [2048], P('rows'), may hold values from 0.0001 to 0.003
Outputs:
- filtered_log: float32 [2048, 106496], P('rows', 'vocab')
- entropy: float32 [2048], P('rows')
Inputs may be any that keep to these rules, and one draw needn't show every extreme that they name: `hidden`: real-valued activations. `head_weight`: real-valued weights.
All inputs are finite; a program needn't handle non-finite values.
Results may differ from a plain program's by a relative error of at most 0.0003.
Values may be sent and summed in bfloat16 or wider, within the bound.
A program may use at most 64 MiB of HBM per device.

v0:
```python
import jax
import jax.numpy as jnp
from jax import lax
from jax.sharding import PartitionSpec as P


def from_everyone(shard, axis):
    peers = lax.axis_size(axis)
    return lax.all_to_all(
        jnp.broadcast_to(shard[None], (peers, *shard.shape)), axis, 0, 0, tiled=True
    )


def all_in_one(shard, axis):
    leaves = jax.tree.leaves(shard)
    sequence = sorted(range(len(leaves)), key=lambda k: -leaves[k].size)
    width = (1, *leaves[sequence[0]].shape)[-1]
    lines = [
        jnp.pad(leaves[k].reshape(-1), (0, -leaves[k].size % width)).reshape(-1, width)
        for k in sequence
    ]
    both, at, found = (from_everyone(jnp.concatenate(lines), axis), 0, {})
    for k, line in zip(sequence, lines):
        piece = both[:, at : at + len(line)].reshape(len(both), -1)
        found[k] = piece[:, : leaves[k].size].reshape(-1, *leaves[k].shape)
        at += len(line)
    numbers = iter(range(len(leaves)))
    return jax.tree.map(lambda _: found[next(numbers)], shard)


def combined_pairwise(pieces, combine):
    while len(jax.tree.leaves(pieces)[0]) > 1:
        pieces = jax.vmap(combine)(
            *(jax.tree.map(lambda part: part[side::2], pieces) for side in (0, 1))
        )
    return jax.tree.map(lambda part: part[0], pieces)


def joined_all(shard, axis, combine):
    pieces = all_in_one(shard, axis)
    return combined_pairwise(pieces, combine)


def over_copies(shard, axis):
    return from_everyone(shard, axis).sum(axis=0)


def combine_parts(first, second):
    first_peak, first_total, first_moment = first
    second_peak, second_total, second_moment = second
    top_peak = jnp.maximum(first_peak, second_peak)
    first_factor = jnp.exp(first_peak - top_peak)
    second_factor = jnp.exp(second_peak - top_peak)
    merged_total = first_total * first_factor + second_total * second_factor
    merged_moment = first_factor * (
        first_moment + (first_peak - top_peak) * first_total
    ) + second_factor * (second_moment + (second_peak - top_peak) * second_total)
    return (top_peak, merged_total, merged_moment)


def shards(hidden, head_weight, eta_level):
    scores = jnp.dot(
        hidden,
        lax.all_gather(head_weight, "rows", axis=1, tiled=True),
        preferred_element_type=jnp.float32,
    )
    local_peak = jnp.max(scores, axis=1)
    shifted = jnp.exp(scores - local_peak[:, None])
    local_total = jnp.sum(shifted, axis=1)
    local_moment = jnp.sum(shifted * (scores - local_peak[:, None]), axis=1)
    row_peak, row_total, moment = joined_all(
        (local_peak, local_total, local_moment), "vocab", combine_parts
    )
    shifted = shifted * jnp.exp(local_peak - row_peak)[:, None]
    entropy = jnp.log(row_total) - moment / row_total
    threshold = jnp.minimum(eta_level, jnp.sqrt(eta_level) * jnp.exp(-entropy))
    row_probs = shifted / row_total[:, None]
    kept_weight = jnp.maximum(row_probs - threshold[:, None], 0.0)
    kept_mass = over_copies(jnp.sum(kept_weight, axis=1), "vocab")
    filtered = jnp.log(kept_weight + 0.001 * threshold[:, None]) - jnp.log(kept_mass)[:, None]
    return (filtered, entropy)


def solution(mesh):
    return jax.shard_map(
        shards,
        mesh=mesh,
        in_specs=(P("rows", None), P(None, ("vocab", "rows")), P("rows")),
        out_specs=(P("rows", "vocab"), P("rows")),
        check_vma=False,
    )
```

profile of v0, /device:TPU:1, one launch (start us, length us, event | category | flops | bytes accessed | tf_op | source)
XLA Modules:
  0.0 188.1 jit_solution(3715837613669904508)
XLA Ops:
  7.2 0.0 copy-start
  7.2 0.0 all-gather.2.cloned.1.call-start
  7.2 0.7 all-gather.2.cloned.1.call-update
  7.9 103.3 %all-gather.2.cloned.1.call-done = bf16[2880,1664]{0,1:T(8,128)(2,1)} async-done(((bf16[2880,416]{0,1:T(8,128)(2,1)}), bf16[2880,1664]{0,1:T(8,128)(2,1)}) %all-gather.2.cloned.1.call-update) | async-done | bytes 9584656 | tf_op jit(solution)/shard_map/all_gather | solution.py:64
  111.2 0.0 copy-done
  111.2 9.8 %fusion.10 = (f32[512]{0:T(512)S(1)}, f32[512,1664]{1,0:T(8,128)S(1)}) fusion(bf16[512,2880]{0,1:T(8,128)(2,1)S(1)} %copy-done, bf16[2880,1664]{0,1:T(8,128)(2,1)} %all-gather.2.cloned.1.call-done), kind=kOutput, calls=%fused_computation.37 | convolution fusion | flops 4908187136 | bytes 15943680 | tf_op jit(solution)/shard_map/dot_general | solution.py:62
  121.0 0.0 copy-start.1
  121.1 1.7 copy-done.1
  122.8 1.0 exponential_reduce_fusion
  123.8 0.0 copy-start.2
  123.8 0.1 broadcast_in_dim.4
  123.9 28.2 %all_to_all.11 = f32[64,3,512]{2,1,0:T(4,128)S(1)} all-to-all(f32[64,3,512]{2,1,0:T(4,128)S(1)} %broadcast_in_dim.4), channel_id=1, replica_groups=mesh['vocab'=64,'rows'=4] {'vocab'}, dimensions={0} | all-to-all | bytes 786432 | tf_op jit(solution)/shard_map/all_to_all | solution.py:9
  152.1 0.3 fusion.9
  152.7 0.7 multiply_add_fusion
  153.4 0.8 slice.153
  154.2 0.8 slice.152
  155.7 0.0 copy-done.2
  155.7 0.6 broadcast_multiply_fusion
  156.3 3.8 %fusion.7 = (f32[512]{0:T(512)S(1)}, f32[512,1664]{1,0:T(8,128)}) fusion(f32[512]{0:T(512)S(1)} %get-tuple-element.5, f32[512]{0:T(512)S(1)} %bitcast.19, f32[512]{0:T(512)S(1)} %subtract_exponential_fusion, f32[512,1664]{1,0:T(8,128)} %copy-done.1, f32[512]{0:T(512)S(1)} %get-tuple-element.24), kind=kLoop, calls=%fused_computation.35 | loop fusion | flops 5111296 | bytes 6825984 | tf_op jit(solution)/shard_map/reduce_sum | solution.py:79
  160.2 0.1 broadcast_in_dim.5
  160.2 16.6 %all_to_all.12 = f32[64,1,512]{2,1,0:T(1,128)S(1)} all-to-all(f32[64,1,512]{2,1,0:T(1,128)S(1)} %broadcast_in_dim.5), channel_id=1, replica_groups=mesh['vocab'=64,'rows'=4] {'vocab'}, dimensions={0} | all-to-all | bytes 262144 | tf_op jit(solution)/shard_map/all_to_all | solution.py:9
  176.9 0.1 reduce_sum.39
  177.0 4.3 %log_subtract_fusion = f32[512,1664]{1,0:T(8,128)} fusion(f32[512,1664]{1,0:T(8,128)} %get-tuple-element.8, f32[512]{0:T(512)S(1)} %log.15, f32[512]{0:T(512)S(1)} %get-tuple-element.4), kind=kLoop, calls=%fused_computation.7 | loop fusion | flops 1703936 | bytes 6819840 | tf_op jit(solution)/shard_map/sub | solution.py:80
  (44 shorter events, 0.9 us)
Async XLA Ops:
  7.2 104.1 %copy-start = (bf16[512,2880]{0,1:T(8,128)(2,1)S(1)}, bf16[512,2880]{0,1:T(8,128)(2,1)}, u32[]{:S(2)}) copy-start(bf16[512,2880]{0,1:T(8,128)(2,1)} %param.3) | copy-start | bytes 8847364
  7.2 104.1 %all-gather.2.cloned.1.call-start = ((), (), s32[]{:S(2)}) async-start(), calls=%async_computation.2 | async-start | bytes 12247040 | tf_op jit(solution)/shard_map/all_gather | solution.py:64
  121.0 1.8 copy-start.1
  123.8 31.9 %copy-start.2 = (f32[512]{0:T(512)S(1)}, f32[512]{0:T(512)}, u32[]{:S(2)}) copy-start(f32[512]{0:T(512)} %param.5) | copy-start | bytes 6148
Sparse Core Ops, SparseCore 0:
  9.8 101.3 all-gather.1
where the time goes:
time: 188 us
  waiting for transfers between devices  104 us (55%)
  blocking collectives  44.8 us (24%)
  between operations  14.2 us (8%)
  other arithmetic  10.7 us (6%)
  matrix products  9.81 us (5%)
  local copies, waits for them, and re-layouts  4.51 us (2%)
    all_gather x1, waiting for transfers between devices, shards(): lax.all_gather(head_weight, 'rows', axis=1, tiled=True)  103 us
    all_to_all x2, blocking collectives, from_everyone(): lax.all_to_all(jnp.broadcast_to(shard[None], (peers, *shard.shape)), axis...  44.8 us
    dot_general x1, matrix products, shards(): jnp.dot(hidden, lax.all_gather(head_weight, 'rows', axis=1, tiled=True),...  9.81 us
    sub x1, other arithmetic, shards(): jnp.log(kept_weight + 0.001 * threshold[:, None])  4.27 us
    reduce_sum x1, other arithmetic, shards(): kept_mass = over_copies(jnp.sum(kept_weight, axis=1), 'vocab')  3.84 us
  transfers between devices with their start and end apart: 1, of which 1 were waited for; matrix products, arithmetic and copies ran while one was open for 0% of the time, Pallas kernels for 0%

commit v1 on v0

--- a/solution.py
+++ b/solution.py
@@ -2,6 +2,22 @@
 import jax.numpy as jnp
 from jax import lax
 from jax.sharding import PartitionSpec as P
+
+
+def gather_around(x, axis, dim):
+    ways, here, step = (lax.axis_size(axis), lax.axis_index(axis), x.shape[dim])
+    lengths = [n * ways if d == dim else n for d, n in enumerate(x.shape)]
+    full = lax.dynamic_update_slice_in_dim(jnp.zeros(lengths, x.dtype), x, here * step, axis=dim)
+    going_up = going_down = x
+    for far in range(1, ways // 2 + 1):
+        going_up = lax.ppermute(going_up, axis, [(d, (d + 1) % ways) for d in range(ways)])
+        full = lax.dynamic_update_slice_in_dim(full, going_up, (here - far) % ways * step, axis=dim)
+        if 2 * far < ways:
+            going_down = lax.ppermute(going_down, axis, [(d, (d - 1) % ways) for d in range(ways)])
+            full = lax.dynamic_update_slice_in_dim(
+                full, going_down, (here + far) % ways * step, axis=dim
+            )
+    return full
 
 
 def from_everyone(shard, axis):
@@ -60,9 +76,7 @@
 
 def shards(hidden, head_weight, eta_level):
     scores = jnp.dot(
-        hidden,
-        lax.all_gather(head_weight, "rows", axis=1, tiled=True),
-        preferred_element_type=jnp.float32,
+        hidden, gather_around(head_weight, "rows", 1), preferred_element_type=jnp.float32
     )
     local_peak = jnp.max(scores, axis=1)
     shifted = jnp.exp(scores - local_peak[:, None])

time: 188 us -> 214 us (1.14)
  local copies, waits for them, and re-layouts: 4.51 us -> 33 us
  between operations: 14.2 us -> 0.85 us
  other arithmetic: 10.7 us -> 19.4 us
  waiting for transfers between devices: 104 us -> 97 us
  blocking collectives: 44.8 us -> 50.9 us
  starting transfers between devices: 0.04 us -> 5.36 us
  matrix products: 9.81 us -> 5.58 us
    all_gather x1 -> x0, waiting for transfers between devices: 103 us -> none  [shards(): lax.all_gather(head_weight, 'rows', axis=1, tiled=True)]
    ppermute x0 -> x3, waiting for transfers between devices: none -> 97 us  [the longest x2 97 us: gather_around(): lax.ppermute(going_up, axis, [(d, (d + 1) % ways) for d in range(ways)])]
    slice x30, local copies, waits for them, and re-layouts: 2.3 us -> 18 us  [combined_pairwise(): part[side::2]]
    dynamic_update_slice x0 -> x4, local copies, waits for them, and re-layouts: none -> 6.42 us  [the longest x2 4.06 us: gather_around(): lax.dynamic_update_slice_in_dim(full, going_up, (here - far) % ways * ste...]
    all_to_all x2, blocking collectives: 44.8 us -> 50.9 us  [from_everyone(): lax.all_to_all(jnp.broadcast_to(shard[None], (peers, *shard.shape)), axis...]
    unnamed x7 -> x20, local copies, waits for them, and re-layouts: 1.77 us -> 7.52 us
    ppermute x0 -> x3, starting transfers between devices: none -> 5.36 us  [the longest x2 4 us: gather_around(): lax.ppermute(going_up, axis, [(d, (d + 1) % ways) for d in range(ways)])]
    add x6, other arithmetic: 0.12 us -> 4.78 us  [combine_parts(): merged_total = first_total * first_factor + second_total * second_factor]
  transfers between devices with their start and end apart: 1 -> 3, of which waited for: 1 -> 2; matrix products, arithmetic and copies ran while one was open for 0% -> 2% of each run, Pallas kernels for 0% -> 0%
where the time goes in v1:
time: 214 us; the launch traced here: 212 us
  waiting for transfers between devices  97 us (45%)
  blocking collectives  50.9 us (24%)
  local copies, waits for them, and re-layouts  33 us (15%)
  other arithmetic  19.4 us (9%)
  matrix products  5.58 us (3%)
  starting transfers between devices  5.36 us (3%)
    ppermute x2, waiting for transfers between devices, gather_around(): lax.ppermute(going_up, axis, [(d, (d + 1) % ways) for d in range(ways)])  97 us
    all_to_all x2, blocking collectives, from_everyone(): lax.all_to_all(jnp.broadcast_to(shard[None], (peers, *shard.shape)), axis...  50.9 us
    slice x30, local copies, waits for them, and re-layouts, combined_pairwise(): part[side::2]  18 us
    unnamed x20, local copies, waits for them, and re-layouts  7.52 us
    dot_general x1, matrix products, shards(): jnp.dot(hidden, gather_around(head_weight, 'rows', 1), preferred_element_...  5.58 us
    sub x1, other arithmetic, shards(): jnp.log(kept_weight + 0.001 * threshold[:, None])  4.91 us
    add x6, other arithmetic, combine_parts(): merged_total = first_total * first_factor + second_total * second_factor  4.78 us
  transfers between devices with their start and end apart: 3, of which 2 were waited for; matrix products, arithmetic and copies ran while one was open for 2% of the time, Pallas kernels for 0%

profile of v1, /device:TPU:1, one launch (start us, length us, event | category | flops | bytes accessed | tf_op | source)
XLA Modules:
  0.0 212.2 jit_solution(1075750705874465031)
XLA Ops:
  0.6 2.1 collective-permute-start
  2.8 1.4 collective-permute-start.1
  4.1 50.8 %collective-permute-done = bf16[2880,416]{0,1:T(8,128)(2,1)} collective-permute-done((bf16[2880,416]{0,1:T(8,128)(2,1)}, bf16[2880,416]{0,1:T(8,128)(2,1)}, u32[]{:S(2)}, u32[]{:S(2)}) %collective-permute-start) | collective-permute-done | bytes 2396192 | tf_op jit(solution)/shard_map/ppermute | solution.py:13
  55.0 1.9 collective-permute-start.2
  57.5 1.0 copy-done.2
  58.9 2.0 constant_dynamic-update-slice_fusion.2
  60.9 2.0 constant_dynamic-update-slice_fusion.1
  62.9 46.2 %collective-permute-done.2 = bf16[2880,416]{0,1:T(8,128)(2,1)} collective-permute-done((bf16[2880,416]{0,1:T(8,128)(2,1)}, bf16[2880,416]{0,1:T(8,128)(2,1)}, u32[]{:S(2)}, u32[]{:S(2)}) %collective-permute-start.2) | collective-permute-done | bytes 2396192 | tf_op jit(solution)/shard_map/ppermute | solution.py:13
  109.2 2.0 constant_dynamic-update-slice_fusion
  111.2 5.6 %fusion.9 = (f32[512]{0:T(512)S(1)}, f32[1664,512]{1,0:T(8,128)S(1)}) fusion(bf16[2880,1664]{0,1:T(8,128)(2,1)S(1)} %constant_dynamic-update-slice_fusion, bf16[512,2880]{0,1:T(8,128)(2,1)S(1)} %copy-done), kind=kOutput, calls=%fused_computation.41 | convolution fusion | flops 4908187136 | bytes 15943680 | tf_op jit(solution)/shard_map/dot_general | solution.py:78
  116.8 1.7 copy-done.1
  119.3 34.3 %all_to_all.11 = f32[64,3,512]{2,1,0:T(4,128)S(1)} all-to-all(f32[64,3,512]{2,1,0:T(4,128)S(1)} %broadcast_in_dim.7), channel_id=1, replica_groups=mesh['vocab'=64,'rows'=4] {'vocab'}, dimensions={0} | all-to-all | bytes 786432 | tf_op jit(solution)/shard_map/all_to_all | solution.py:25
  154.8 0.9 slice.139
  157.9 1.4 slice.129
  159.2 1.4 slice.141
  160.6 1.4 slice.142
  162.0 1.4 multiply_add_fusion.5
  163.3 1.3 slice.130
  164.7 1.3 slice.131
  166.0 1.3 slice.143
  167.3 1.3 slice.144
  168.6 1.4 multiply_add_fusion.7
  170.0 1.3 slice.132
  171.3 1.3 slice.133
  172.6 1.3 slice.145
  173.9 1.3 slice.146
  175.9 0.9 multiply_add_fusion
  181.6 1.3 broadcast_multiply_fusion
  182.9 2.9 %fusion.4 = f32[512]{0:T(512)S(1)} fusion(f32[512]{0:T(512)S(1)} %get-tuple-element.11, f32[512]{0:T(512)S(1)} %bitcast.27, f32[512]{0:T(512)S(1)} %subtract_exponential_fusion, f32[1664,512]{1,0:T(8,128)} %copy-done.1, f32[512]{0:T(512)} %copy-done.7), kind=kLoop, calls=%fused_computation.8 | loop fusion | flops 5111296 | bytes 3418112 | tf_op jit(solution)/shard_map/reduce_sum | solution.py:93
  185.8 16.6 %all_to_all.12 = f32[64,1,512]{2,1,0:T(1,128)S(1)} all-to-all(f32[64,1,512]{2,1,0:T(1,128)S(1)} %broadcast_in_dim.8), channel_id=1, replica_groups=mesh['vocab'=64,'rows'=4] {'vocab'}, dimensions={0} | all-to-all | bytes 262144 | tf_op jit(solution)/shard_map/all_to_all | solution.py:25
  202.6 4.9 %log_subtract_fusion = f32[512,1664]{0,1:T(8,128)} fusion(f32[512]{0:T(512)S(1)} %log.15, f32[512]{0:T(512)S(1)} %get-tuple-element.10, f32[512]{0:T(512)S(1)} %get-tuple-element.11, f32[512]{0:T(512)S(1)} %bitcast.28, f32[512]{0:T(512)S(1)} %subtract_exponential_fusion, f32[1664,512]{1,0:T(8,128)} %copy-done.1, f32[512]{0:T(512)S(1)} %copy-done.8), kind=kLoop, calls=%fused_computation.7 | loop fusion | flops 5963776 | bytes 6828032 | tf_op jit(solution)/shard_map/sub | solution.py:94
  207.5 4.7 %copy.14 = f32[512,1664]{1,0:T(8,128)} copy(f32[512,1664]{0,1:T(8,128)} %log_subtract_fusion) | data formatting | bytes 6815744
  (56 shorter events, 10.9 us)
Async XLA Ops:
  0.6 110.6 %copy-start = (bf16[512,2880]{0,1:T(8,128)(2,1)S(1)}, bf16[512,2880]{0,1:T(8,128)(2,1)}, u32[]{:S(2)}) copy-start(bf16[512,2880]{0,1:T(8,128)(2,1)} %param.3) | copy-start | bytes 8847364
  0.6 54.3 %collective-permute-start = (bf16[2880,416]{0,1:T(8,128)(2,1)}, bf16[2880,416]{0,1:T(8,128)(2,1)}, u32[]{:S(2)}, u32[]{:S(2)}) collective-permute-start(bf16[2880,416]{0,1:T(8,128)(2,1)} %param.4), channel_id=1, source_target_pairs={{0,1},{1,2},{2,3},{3,0},{4,5},{5,6},{6,7},{7,4},{8,9},{9,10},{10,1... | collective-permute-start | bytes 7188488 | tf_op jit(solution)/shard_map/ppermute | solution.py:13
  2.8 58.1 %collective-permute-start.1 = (bf16[2880,416]{0,1:T(8,128)(2,1)}, bf16[2880,416]{0,1:T(8,128)(2,1)}, u32[]{:S(2)}, u32[]{:S(2)}) collective-permute-start(bf16[2880,416]{0,1:T(8,128)(2,1)} %param.4), channel_id=1, source_target_pairs={{0,3},{1,0},{2,1},{3,2},{4,7},{5,4},{6,5},{7,6},{8,11},{9,8},{10,9... | collective-permute-start | bytes 7188488 | tf_op jit(solution)/shard_map/ppermute | solution.py:16
  55.0 54.2 %collective-permute-start.2 = (bf16[2880,416]{0,1:T(8,128)(2,1)}, bf16[2880,416]{0,1:T(8,128)(2,1)}, u32[]{:S(2)}, u32[]{:S(2)}) collective-permute-start(bf16[2880,416]{0,1:T(8,128)(2,1)} %collective-permute-done), channel_id=1, source_target_pairs={{0,1},{1,2},{2,3},{3,0},{4,5},{5,6},{6,7},{7,4},{8,9},{9,10},{10,1... | collective-permute-start | bytes 7188488 | tf_op jit(solution)/shard_map/ppermute | solution.py:13
  56.8 1.7 copy-start.2
  116.8 1.8 copy-start.1
  116.8 37.1 %copy-start.7 = (f32[512]{0:T(512)}, f32[512]{0:T(512)S(1)}, u32[]{:S(2)}) copy-start(f32[512]{0:T(512)S(1)} %get-tuple-element.28) | copy-start | bytes 6148
  154.7 20.4 %copy-start.3 = (f32[16,512]{1,0:T(8,128)}, f32[16,512]{1,0:T(8,128)S(1)}, u32[]{:S(2)}) copy-start(f32[16,512]{1,0:T(8,128)S(1)} %slice.126) | copy-start | bytes 98308
  154.7 20.4 %copy-start.4 = (f32[16,512]{1,0:T(8,128)}, f32[16,512]{1,0:T(8,128)S(1)}, u32[]{:S(2)}) copy-start(f32[16,512]{1,0:T(8,128)S(1)} %slice.127) | copy-start | bytes 98308
  155.6 19.5 %copy-start.5 = (f32[16,512]{1,0:T(8,128)}, f32[16,512]{1,0:T(8,128)S(1)}, u32[]{:S(2)}) copy-start(f32[16,512]{1,0:T(8,128)S(1)} %slice.139) | copy-start | bytes 98308
  156.5 18.7 %copy-start.6 = (f32[16,512]{1,0:T(8,128)}, f32[16,512]{1,0:T(8,128)S(1)}, u32[]{:S(2)}) copy-start(f32[16,512]{1,0:T(8,128)S(1)} %slice.140) | copy-start | bytes 98308
  175.9 26.7 %copy-start.8 = (f32[512]{0:T(512)S(1)}, f32[512]{0:T(512)}, u32[]{:S(2)}) copy-start(f32[512]{0:T(512)} %copy-done.7) | copy-start | bytes 6148
